TPU v7x, 32 devices: a whole 2x2x4 slice. The times are simulated.
32 devices in a mesh: sec: 4 (over x, core), row: 4 (over z), col: 2 (over y).
Axes of the slice: x: 2, y: 2, z: 4, core: 2. Of those that a mesh axis runs over, the one named last changes fastest.
Arguments:
- amplitudes: bfloat16 [4, 2, 512, 8192], P('sec', None, 'row', 'col'), may hold values from -0.25 to 0.25, as said below
- state_energies: float32 [4, 8192], P('sec', 'col'), may hold values from 1.25 to 12
- radii_table: int32 [5], replicated, may hold values from 20 to 84, as said below
- plan: int32 [4, 2], P('sec'), may hold values from 0 to 31, as said below
- entry_r: float32 [4, 512, 512], P('sec', 'col', 'row'), may hold values from -16 to 48, as said below
- fresh_r: float32 [1, 512, 512], P(None, 'col', 'row'), may hold values from -16 to 48, as said below
Outputs:
- exit_r: float32 [2, 4, 512, 512], P(None, 'sec', 'col', 'row')
Inputs may be any that keep to these rules, and one draw needn't show every extreme that they name: Each sector's outer-boundary amplitudes are correlated with its inner-boundary ones. `radii_table`: strictly increasing; consecutive radii differ by 4 to 16; the first is at least 20 and the last equals 84. plan[s, t] equals plan[s-1, t-1] for s, t >= 1. `entry_r`: symmetric positive definite, every eigenvalue at least 0.5. `fresh_r`: symmetric positive definite, every eigenvalue at least 0.5.
All inputs are finite; a program needn't handle non-finite values.
Results may differ from a plain program's by a relative error of at most 0.0016.
Values may be sent and summed in bfloat16 or wider, within the bound.
A program may use at most 64 MiB of HBM per device.

v0:
```python
import functools
import jax
import jax.numpy as jnp
from jax import lax
from jax.experimental import pallas as pl
from jax.experimental.pallas import tpu as pltpu
from jax.sharding import PartitionSpec as P

ENERGIES = 32
TICKS = 2
BLOCK = 128
SUB = 8
HIGHEST = lax.Precision.HIGHEST


MESH = pl.DeviceIdType.MESH


def worker(sector):
    return sector % 2


def span(block, blocks):
    if block < blocks // 2:
        return block, 0, (blocks - block) * BLOCK
    mate = blocks - 1 - block
    return mate, (blocks - mate) * BLOCK, (blocks - block) * BLOCK


def inverse_factor(block):
    size = block.shape[0]
    groups = size // SUB
    sub_rows = lax.broadcasted_iota(jnp.int32, (SUB, size), 0)
    left = block
    right = jnp.where(
        lax.broadcasted_iota(jnp.int32, (size, size), 0)
        == lax.broadcasted_iota(jnp.int32, (size, size), 1),
        1.0,
        0.0,
    )
    done = []
    for g in range(groups):
        base = SUB * g
        u, v = left[:SUB], right[:SUB]
        cols = [jnp.broadcast_to(u[:, base + q : base + q + 1], (SUB, size)) for q in range(SUB)]
        scale = jnp.zeros((SUB, size), jnp.float32)
        for p in range(SUB):
            pivot = cols[p][p : p + 1, :]
            scale = jnp.where(sub_rows == p, pivot, scale)
            if p + 1 < SUB:
                f = jnp.where(sub_rows > p, cols[p] / pivot, 0.0)
                u = u - f * u[p : p + 1, :]
                v = v - f * v[p : p + 1, :]
                for q in range(p + 1, SUB):
                    cols[q] = cols[q] - f * cols[q][p : p + 1, :]
        scale = lax.rsqrt(scale)
        u = u * scale
        v = v * scale
        done.append(v)
        if g + 1 < groups:
            turned = u.T[base + SUB :, :]
            left, right = left[SUB:], right[SUB:]
            for q in range(SUB):
                c = jnp.broadcast_to(turned[:, q : q + 1], turned.shape[:1] + (size,))
                left = left - c * u[q : q + 1, :]
                right = right - c * v[q : q + 1, :]
    return jnp.concatenate(done, 0)


def gather_kernel(
    rows, cols, sectors, amp_ref, weight_ref, tile_ref, out_ref,
    panels, weights, tiles, scaled, parts, arrived, work, factor_ref, full, upper, inbox,
    amp_send, amp_recv, small_send, small_recv, sum_send, sum_recv,
    tile_send, tile_recv, shift_send, shift_recv,
):
    row, col = lax.axis_index("row"), lax.axis_index("col")
    sec = lax.axis_index("sec")
    home = worker(sec)
    root = (rows - 1) // 2
    chunk = weight_ref.shape[1]
    row_block = amp_ref.shape[1]
    tile_rows = tile_ref.shape[1]
    channels = panels.shape[1]
    blocks = 2 * channels // BLOCK
    at_home = col == home
    at_root = at_home & (row == root)

    barrier = pltpu.get_barrier_semaphore()
    for r in range(rows):
        for c in range(cols):

            @pl.when((row != r) | (col != c))
            def _():
                pl.semaphore_signal(
                    barrier, inc=1, device_id={"row": r, "col": c}, device_id_type=MESH
                )

    for step in (-1, 1):

        @pl.when(at_root & (sec + step >= 0) & (sec + step < sectors))
        def _():
            pl.semaphore_signal(
                barrier,
                inc=1,
                device_id={"sec": sec + step, "col": worker(sec + step + 2)},
                device_id_type=MESH,
            )

    before = jnp.where(at_root & (sec > 0), 1, 0)
    after = jnp.where(at_root & (sec < sectors - 1), 1, 0)
    pl.semaphore_wait(barrier, rows * cols - 1 + before + after)

    my_rows = pl.ds(pl.multiple_of(row * row_block, row_block), row_block)
    my_states = pl.ds(pl.multiple_of(col * chunk, chunk), chunk)
    my_tile = pl.ds(pl.multiple_of(col * tile_rows, tile_rows), tile_rows)
    source = row * cols + col

    def amp_there(r):
        return pltpu.make_async_remote_copy(
            src_ref=amp_ref.at[:, :, pl.ds(r * chunk, chunk)],
            dst_ref=panels.at[:, my_rows, my_states],
            send_sem=amp_send.at[r],
            recv_sem=amp_recv.at[source],
            device_id={"row": r, "col": home},
            device_id_type=MESH,
        )

    def amp_here(r):
        return pltpu.make_async_copy(
            amp_ref.at[:, :, pl.ds(r * chunk, chunk)],
            panels.at[:, my_rows, my_states],
            amp_send.at[r],
        )

    def small_there(src, dst, i):
        return pltpu.make_async_remote_copy(
            src_ref=src,
            dst_ref=dst,
            send_sem=small_send.at[i],
            recv_sem=small_recv.at[i, col],
            device_id={"col": home},
            device_id_type=MESH,
        )

    smalls = [
        (weight_ref, weights.at[:, my_states]),
        (tile_ref, tiles.at[:, my_tile, :]),
    ]
    for i, (src, dst) in enumerate(smalls):

        @pl.when(at_home)
        def _():
            pltpu.make_async_copy(src, dst, small_send.at[i]).start()

        @pl.when(jnp.logical_not(at_home))
        def _():
            small_there(src, dst, i).start()

    for r in range(rows):
        here = at_home & (row == r)

        @pl.when(here)
        def _():
            amp_here(r).start()

        @pl.when(jnp.logical_not(here))
        def _():
            amp_there(r).start()

    for i, (src, dst) in enumerate(smalls):

        @pl.when(at_home)
        def _():
            pltpu.make_async_copy(src, dst, small_send.at[i]).wait()

        @pl.when(jnp.logical_not(at_home))
        def _():
            small_there(src, dst, i).wait_send()

    for r in range(rows):
        here = at_home & (row == r)

        @pl.when(here)
        def _():
            amp_here(r).wait()

        @pl.when(jnp.logical_not(here))
        def _():
            amp_there(r).wait_send()

    half = BLOCK // 2
    pieces = [(pair, h) for pair in range(blocks // 2) for h in range(2)]

    def piece_copy(period, i, side):
        pair, h = pieces[i]
        return pltpu.make_async_remote_copy(
            src_ref=parts.at[period, pair, pl.ds(h * half, half)],
            dst_ref=arrived.at[period, side, pair, pl.ds(h * half, half)],
            send_sem=sum_send.at[period, i],
            recv_sem=sum_recv.at[period, side, i],
            device_id={"row": row - 1 if side == 0 else row + 1},
            device_id_type=MESH,
        )

    def piece_arrival(period, i, side):
        pair, h = pieces[i]
        return pltpu.make_async_remote_copy(
            src_ref=parts.at[period, pair, pl.ds(h * half, half)],
            dst_ref=arrived.at[period, side, pair, pl.ds(h * half, half)],
            send_sem=sum_send.at[period, i],
            recv_sem=sum_recv.at[period, side, i],
            device_id={"row": row + 1 if side == 0 else row - 1},
            device_id_type=MESH,
        )

    def pass_on(period, side, inner):
        for i, (pair, h) in enumerate(pieces):
            at = slice(h * half, (h + 1) * half)

            @pl.when(inner)
            def _():
                piece_arrival(period, i, side).wait_recv()
                parts[period, pair, at, :] += arrived[period, side, pair, at, :]

            piece_copy(period, i, side).start()
        for i in range(len(pieces)):
            piece_copy(period, i, side).wait_send()

    def take_sums(period):
        for pair in range(blocks // 2):
            for h in range(2):
                i = 2 * pair + h
                if root < rows - 1:
                    piece_arrival(period, i, 0).wait_recv()
                if root > 0:
                    piece_arrival(period, i, 1).wait_recv()
            for block in (pair, blocks - 1 - pair):
                _, start, wide = span(block, blocks)
                total = parts[period, pair, :, start : start + wide]
                if root < rows - 1:
                    total = total + arrived[period, 0, pair, :, start : start + wide]
                if root > 0:
                    total = total + arrived[period, 1, pair, :, start : start + wide]
                work[block * BLOCK : (block + 1) * BLOCK, block * BLOCK :] = total

    half_blocks = blocks // 2

    def shift_copy(step):
        return pltpu.make_async_remote_copy(
            src_ref=upper,
            dst_ref=inbox,
            send_sem=shift_send,
            recv_sem=shift_recv,
            device_id={"sec": sec + step, "col": worker(sec + step + 2)},
            device_id_type=MESH,
        )

    def tile_copy(period, r, c):
        return pltpu.make_async_remote_copy(
            src_ref=full.at[period, pl.ds(c * tile_rows, tile_rows), pl.ds(r * row_block, row_block)],
            dst_ref=out_ref.at[period],
            send_sem=tile_send.at[period, r * cols + c],
            recv_sem=tile_recv.at[period],
            device_id={"row": r, "col": c},
            device_id_type=MESH,
        )

    def tile_here(period, c):
        return pltpu.make_async_copy(
            full.at[period, pl.ds(c * tile_rows, tile_rows), pl.ds(root * row_block, row_block)],
            out_ref.at[period],
            tile_send.at[period, root * cols + c],
        )

    def each_tile(period, there, here):
        for c in range(cols):
            for r in range(rows):
                if r == root:

                    @pl.when(col == c)
                    def _():
                        here(tile_here(period, c))

                    @pl.when(col != c)
                    def _():
                        there(tile_copy(period, r, c))

                else:
                    there(tile_copy(period, r, c))

    def eliminate(period):
        def step(k, carry):
            lo = pl.multiple_of(k * BLOCK, BLOCK)
            factor_ref[...] = inverse_factor(work[pl.ds(lo, BLOCK), pl.ds(lo, BLOCK)])
            for j in range(half_blocks):

                @pl.when(k == j)
                def _():
                    hi = (j + 1) * BLOCK
                    solved = jnp.dot(
                        factor_ref[...],
                        work[j * BLOCK : hi, hi:],
                        precision=HIGHEST,
                        preferred_element_type=jnp.float32,
                    )
                    for i in range(hi, 2 * channels, BLOCK):
                        work[i : i + BLOCK, i:] -= lax.dot_general(
                            solved[:, i - hi : i - hi + BLOCK],
                            solved[:, i - hi :],
                            (((0,), (0,)), ((), ())),
                            precision=HIGHEST,
                            preferred_element_type=jnp.float32,
                        )

            return carry

        lax.fori_loop(0, half_blocks, step, 0)
        for i in range(half_blocks):
            lo = channels + i * BLOCK
            pair, start, wide = span(i, half_blocks)

            @pl.when(period == 0)
            def _():
                upper[pair, :, start : start + wide] = work[lo : lo + BLOCK, lo:]

            for j in range(i, half_blocks):
                at = channels + j * BLOCK
                tile = work[lo : lo + BLOCK, at : at + BLOCK]
                full[period, i * BLOCK : (i + 1) * BLOCK, j * BLOCK : (j + 1) * BLOCK] = tile
                if j > i:
                    full[period, j * BLOCK : (j + 1) * BLOCK, i * BLOCK : (i + 1) * BLOCK] = tile.T

    def greens(period):
        weight = weights[pl.ds(period, 1), :]
        for side in range(2):
            scaled[side] = (panels[side].astype(jnp.float32) * weight).astype(jnp.bfloat16)
        contraction = (((1,), (1,)), ((), ()))
        for left, right, first_block, first_column in (
            (0, 0, 0, 0),
            (0, 1, 0, channels),
            (1, 1, channels // BLOCK, channels),
        ):
            for i in range(0, channels, 2 * BLOCK):
                begin = i if left == right else 0
                green = lax.dot_general(
                    scaled[left, i : i + 2 * BLOCK, :],
                    panels[right, begin:, :],
                    contraction,
                    preferred_element_type=jnp.float32,
                )
                for j in range(2):
                    block = first_block + i // BLOCK + j
                    pair, start, _ = span(block, blocks)
                    skip = j * BLOCK if left == right else 0
                    at = start + first_column + begin + skip - block * BLOCK
                    wide = channels - begin - skip
                    parts[period, pair, :, at : at + wide] = green[
                        j * BLOCK : (j + 1) * BLOCK, skip:
                    ]
        for r in range(rows):

            @pl.when(row == r)
            def _():
                for block in range(r + 1):
                    pair, start, _ = span(block, blocks)
                    at = start + (r - block) * BLOCK
                    parts[period, pair, :, at : at + BLOCK] += tiles[
                        period, block * BLOCK : (block + 1) * BLOCK, :
                    ]

    @pl.when(at_home)
    def _():
        for c in range(cols):

            @pl.when(col != c)
            def _():
                for i in range(2):
                    dst = (
                        weights.at[:, pl.ds(c * chunk, chunk)],
                        tiles.at[:, pl.ds(c * tile_rows, tile_rows), :],
                    )[i]
                    pltpu.make_async_remote_copy(
                        src_ref=dst, dst_ref=dst, send_sem=small_send.at[i],
                        recv_sem=small_recv.at[i, c], device_id={"col": c}, device_id_type=MESH,
                    ).wait_recv()

            for r in range(rows):

                @pl.when((row != r) | (col != c))
                def _():
                    dst = panels.at[
                        :, pl.ds(r * row_block, row_block), pl.ds(c * chunk, chunk)
                    ]
                    pltpu.make_async_remote_copy(
                        src_ref=dst, dst_ref=dst, send_sem=amp_send.at[0],
                        recv_sem=amp_recv.at[r * cols + c], device_id={"row": r, "col": c},
                        device_id_type=MESH,
                    ).wait_recv()

        def tick(period, carry):
            greens(period)

            @pl.when(row > root)
            def _():
                pass_on(period, 0, row < rows - 1)

            @pl.when(row < root)
            def _():
                pass_on(period, 1, row > 0)

            @pl.when(row == root)
            def _():
                take_sums(period)

                @pl.when((period > 0) & (sec > 0))
                def _():
                    shift_copy(-1).wait_recv()
                    for k in range(half_blocks):
                        pair, start, wide = span(k, half_blocks)
                        work[k * BLOCK : (k + 1) * BLOCK, k * BLOCK : channels] += inbox[
                            pair, :, start : start + wide
                        ]

                eliminate(period)

                @pl.when((period == 0) & (sec < sectors - 1))
                def _():
                    shift_copy(1).start()

                each_tile(period, lambda copy: copy.start(), lambda copy: copy.start())

            return carry

        lax.fori_loop(0, TICKS, tick, 0)

    @pl.when(at_root)
    def _():
        @pl.when(sec < sectors - 1)
        def _():
            shift_copy(1).wait_send()

        for period in range(TICKS):
            each_tile(period, lambda copy: copy.wait_send(), lambda copy: copy.wait())

    @pl.when(jnp.logical_not(at_root))
    def _():
        for period in range(TICKS):
            pltpu.make_async_remote_copy(
                src_ref=out_ref.at[period],
                dst_ref=out_ref.at[period],
                send_sem=tile_send.at[period, 0],
                recv_sem=tile_recv.at[period],
                device_id={"row": root, "col": home},
                device_id_type=MESH,
            ).wait_recv()


def gather(panels, weight, tiles, rows, cols, sectors):
    _, row_block, states = panels.shape
    chunk = states // rows
    channels = rows * row_block
    pairs = channels // BLOCK
    width = (2 * pairs + 1) * BLOCK
    assert row_block == BLOCK and TICKS == 2
    vmem = pl.BlockSpec(memory_space=pltpu.VMEM)
    dma = pltpu.SemaphoreType.DMA
    f32, bf16 = jnp.float32, jnp.bfloat16
    packed = pltpu.VMEM((pairs // 2, BLOCK, (pairs + 1) * BLOCK), f32)
    return pl.pallas_call(
        functools.partial(gather_kernel, rows, cols, sectors),
        out_shape=jax.ShapeDtypeStruct(tiles.shape, f32),
        in_specs=[pl.BlockSpec(memory_space=pl.ANY), vmem, vmem],
        out_specs=vmem,
        scratch_shapes=[
            pltpu.VMEM((2, channels, cols * chunk), bf16),
            pltpu.VMEM((weight.shape[0], cols * chunk), f32),
            pltpu.VMEM((TICKS, channels, BLOCK), f32),
            pltpu.VMEM((2, channels, cols * chunk), bf16),
            pltpu.VMEM((TICKS, pairs, BLOCK, width), f32),
            pltpu.VMEM((TICKS, 2, pairs, BLOCK, width), f32),
            pltpu.VMEM((2 * channels, 2 * channels), f32),
            pltpu.VMEM((BLOCK, BLOCK), f32),
            pltpu.VMEM((TICKS, channels, channels), f32),
            packed,
            packed,
            dma((rows,)),
            dma((rows * cols,)),
            dma((2,)),
            dma((2, cols)),
            dma((TICKS, 2 * pairs)),
            dma((TICKS, 2, 2 * pairs)),
            dma((TICKS, rows * cols)),
            dma((TICKS,)),
            dma,
            dma,
        ],
        compiler_params=pltpu.CompilerParams(
            collective_id=0, has_side_effects=True, vmem_limit_bytes=52 * 1024 * 1024
        ),
        name="sectors",
    )(panels, weight, tiles)


def local(amplitudes, state_energies, radii_table, plan, entry_r, fresh_r):
    sec_index = lax.axis_index("sec")
    row_index = lax.axis_index("row")
    sectors, rows, cols = (lax.axis_size(axis) for axis in ("sec", "row", "col"))
    panels = amplitudes[0]
    chunk = panels.shape[2] // rows
    levels = lax.dynamic_slice_in_dim(state_energies[0], row_index * chunk, chunk)
    bounds = lax.dynamic_slice_in_dim(radii_table, sec_index, 2)
    sector_width = (bounds[1] - bounds[0]).astype(jnp.float32)
    energies = plan[0].astype(jnp.float32) / ENERGIES
    weight = 8.0 / (sector_width * (levels[None, :] - energies[:, None]))
    weight = jnp.pad(weight, ((0, SUB - TICKS), (0, 0)))
    tiles = jnp.concatenate([entry_r, jnp.where(sec_index == 0, fresh_r, 0.0)], 0)
    return gather(panels, weight, tiles, rows, cols, sectors)[:, None]


def solution(mesh):
    placed = (
        P("sec", None, "row", "col"),
        P("sec", "col"),
        P(),
        P("sec", None),
        P("sec", "col", "row"),
        P(None, "col", "row"),
    )
    return jax.shard_map(
        local, mesh=mesh, in_specs=placed, out_specs=P(None, "sec", "col", "row"), check_vma=False
    )
```

profile of v0, /device:TPU:29, one launch (start us, length us, event | category | flops | bytes accessed | tf_op | source)
XLA Modules:
  0.0 165.9 jit_solution(10989269449648964747)
XLA Ops:
  0.0 0.0 copy-start
  0.0 0.7 dynamic_slice.6
  0.7 0.7 multiply_bitcast_fusion
  1.4 0.6 fusion
  3.3 0.0 copy-done
  3.3 0.1 multiply_divide_fusion
  3.5 0.9 pad_maximum_fusion.tile_ref
  4.4 160.8 %sectors.1 = f32[2,256,128]{2,1,0:T(8,128)S(1)} custom-call(bf16[2,128,4096]{2,1,0:T(8,128)(2,1)} %bitcast.9, f32[8,1024]{1,0:T(8,128)S(1)} %pad.4.weight_ref, f32[2,256,128]{2,1,0:T(8,128)S(1)} %pad_maximum_fusion.tile_ref), custom_call_target="tpu_custom_call" | custom-call | tf_op jit(solution)/shard_map/sectors/pallas_call | solution.py:469
  165.2 0.7 copy.9
  (3 shorter events, 0.0 us)
Async XLA Ops:
  0.0 3.3 %copy-start = (f32[1,4096]{1,0:T(1,128)S(1)}, f32[1,4096]{1,0:T(1,128)}, u32[]{:S(2)}) copy-start(f32[1,4096]{1,0:T(1,128)} %param.7) | copy-start | bytes 49156
where the time goes:
time: 166 us
  Pallas kernels  161 us (97%)
  local copies, waits for them, and re-layouts  2.07 us (1%)
  other arithmetic  1.69 us (1%)
    pallas_call x1, Pallas kernels, gather(): pl.pallas_call(functools.partial(gather_kernel, rows, cols, sectors), out...  161 us

commit v1 on v0

--- a/solution.py
+++ b/solution.py
@@ -25,6 +25,18 @@
         return block, 0, (blocks - block) * BLOCK
     mate = blocks - 1 - block
     return mate, (blocks - mate) * BLOCK, (blocks - block) * BLOCK
+
+
+def piece_list(blocks):
+    pieces, of_block = [], []
+    for block in range(blocks):
+        pair, start, wide = span(block, blocks)
+        mine = []
+        for first in range(0, wide, 4 * BLOCK):
+            mine.append(len(pieces))
+            pieces.append((pair, start + first, min(4 * BLOCK, wide - first)))
+        of_block.append(mine)
+    return pieces, of_block
 
 
 def inverse_factor(block):
@@ -188,14 +200,13 @@
         def _():
             amp_there(r).wait_send()
 
-    half = BLOCK // 2
-    pieces = [(pair, h) for pair in range(blocks // 2) for h in range(2)]
+    pieces, of_block = piece_list(blocks)
 
     def piece_copy(period, i, side):
-        pair, h = pieces[i]
+        pair, first, wide = pieces[i]
         return pltpu.make_async_remote_copy(
-            src_ref=parts.at[period, pair, pl.ds(h * half, half)],
-            dst_ref=arrived.at[period, side, pair, pl.ds(h * half, half)],
+            src_ref=parts.at[period, pair, :, pl.ds(first, wide)],
+            dst_ref=arrived.at[period, side, pair, :, pl.ds(first, wide)],
             send_sem=sum_send.at[period, i],
             recv_sem=sum_recv.at[period, side, i],
             device_id={"row": row - 1 if side == 0 else row + 1},
@@ -203,10 +214,10 @@
         )
 
     def piece_arrival(period, i, side):
-        pair, h = pieces[i]
+        pair, first, wide = pieces[i]
         return pltpu.make_async_remote_copy(
-            src_ref=parts.at[period, pair, pl.ds(h * half, half)],
-            dst_ref=arrived.at[period, side, pair, pl.ds(h * half, half)],
+            src_ref=parts.at[period, pair, :, pl.ds(first, wide)],
+            dst_ref=arrived.at[period, side, pair, :, pl.ds(first, wide)],
             send_sem=sum_send.at[period, i],
             recv_sem=sum_recv.at[period, side, i],
             device_id={"row": row + 1 if side == 0 else row - 1},
@@ -214,43 +225,40 @@
         )
 
     def pass_on(period, side, inner):
-        for i, (pair, h) in enumerate(pieces):
-            at = slice(h * half, (h + 1) * half)
+        for i, (pair, first, wide) in enumerate(pieces):
+            at = slice(first, first + wide)
 
             @pl.when(inner)
             def _():
                 piece_arrival(period, i, side).wait_recv()
-                parts[period, pair, at, :] += arrived[period, side, pair, at, :]
+                parts[period, pair, :, at] += arrived[period, side, pair, :, at]
 
             piece_copy(period, i, side).start()
         for i in range(len(pieces)):
             piece_copy(period, i, side).wait_send()
 
-    def take_sums(period):
-        for pair in range(blocks // 2):
-            for h in range(2):
-                i = 2 * pair + h
-                if root < rows - 1:
-                    piece_arrival(period, i, 0).wait_recv()
-                if root > 0:
-                    piece_arrival(period, i, 1).wait_recv()
-            for block in (pair, blocks - 1 - pair):
-                _, start, wide = span(block, blocks)
-                total = parts[period, pair, :, start : start + wide]
-                if root < rows - 1:
-                    total = total + arrived[period, 0, pair, :, start : start + wide]
-                if root > 0:
-                    total = total + arrived[period, 1, pair, :, start : start + wide]
-                work[block * BLOCK : (block + 1) * BLOCK, block * BLOCK :] = total
+    def take_sums(period, block):
+        for i in of_block[block]:
+            pair, first, wide = pieces[i]
+            total = parts[period, pair, :, first : first + wide]
+            if root < rows - 1:
+                piece_arrival(period, i, 0).wait_recv()
+                total = total + arrived[period, 0, pair, :, first : first + wide]
+            if root > 0:
+                piece_arrival(period, i, 1).wait_recv()
+                total = total + arrived[period, 1, pair, :, first : first + wide]
+            at = block * BLOCK + first - span(block, blocks)[1]
+            work[block * BLOCK : (block + 1) * BLOCK, at : at + wide] += total
 
     half_blocks = blocks // 2
 
-    def shift_copy(step):
+    def shift_copy(k, step):
+        pair, start, wide = span(k, half_blocks)
         return pltpu.make_async_remote_copy(
-            src_ref=upper,
-            dst_ref=inbox,
-            send_sem=shift_send,
-            recv_sem=shift_recv,
+            src_ref=upper.at[pair, :, pl.ds(start, wide)],
+            dst_ref=inbox.at[pair, :, pl.ds(start, wide)],
+            send_sem=shift_send.at[k],
+            recv_sem=shift_recv.at[k],
             device_id={"sec": sec + step, "col": worker(sec + step + 2)},
             device_id_type=MESH,
         )
@@ -289,7 +297,27 @@
                     there(tile_copy(period, r, c))
 
     def eliminate(period):
+        for block in range(blocks):
+            wide = (blocks - block) * BLOCK
+            work[block * BLOCK : (block + 1) * BLOCK, block * BLOCK :] = jnp.zeros(
+                (BLOCK, wide), jnp.float32
+            )
+
         def step(k, carry):
+            for j in range(half_blocks):
+
+                @pl.when(k == j)
+                def _():
+                    take_sums(period, j)
+
+                @pl.when((k == j) & (period > 0) & (sec > 0))
+                def _():
+                    shift_copy(j, -1).wait_recv()
+                    pair, start, wide = span(j, half_blocks)
+                    work[j * BLOCK : (j + 1) * BLOCK, j * BLOCK : channels] += inbox[
+                        pair, :, start : start + wide
+                    ]
+
             lo = pl.multiple_of(k * BLOCK, BLOCK)
             factor_ref[...] = inverse_factor(work[pl.ds(lo, BLOCK), pl.ds(lo, BLOCK)])
             for j in range(half_blocks):
@@ -316,12 +344,17 @@
 
         lax.fori_loop(0, half_blocks, step, 0)
         for i in range(half_blocks):
+            take_sums(period, half_blocks + i)
             lo = channels + i * BLOCK
             pair, start, wide = span(i, half_blocks)
 
             @pl.when(period == 0)
             def _():
                 upper[pair, :, start : start + wide] = work[lo : lo + BLOCK, lo:]
+
+            @pl.when((period == 0) & (sec < sectors - 1))
+            def _():
+                shift_copy(i, 1).start()
 
             for j in range(i, half_blocks):
                 at = channels + j * BLOCK
@@ -397,8 +430,18 @@
                         device_id_type=MESH,
                     ).wait_recv()
 
+        def own_greens(period, carry):
+            greens(period)
+            return carry
+
+        @pl.when(row == root)
+        def _():
+            lax.fori_loop(0, TICKS, own_greens, 0)
+
         def tick(period, carry):
-            greens(period)
+            @pl.when(row != root)
+            def _():
+                greens(period)
 
             @pl.when(row > root)
             def _():
@@ -410,23 +453,7 @@
 
             @pl.when(row == root)
             def _():
-                take_sums(period)
-
-                @pl.when((period > 0) & (sec > 0))
-                def _():
-                    shift_copy(-1).wait_recv()
-                    for k in range(half_blocks):
-                        pair, start, wide = span(k, half_blocks)
-                        work[k * BLOCK : (k + 1) * BLOCK, k * BLOCK : channels] += inbox[
-                            pair, :, start : start + wide
-                        ]
-
                 eliminate(period)
-
-                @pl.when((period == 0) & (sec < sectors - 1))
-                def _():
-                    shift_copy(1).start()
-
                 each_tile(period, lambda copy: copy.start(), lambda copy: copy.start())
 
             return carry
@@ -437,7 +464,8 @@
     def _():
         @pl.when(sec < sectors - 1)
         def _():
-            shift_copy(1).wait_send()
+            for k in range(half_blocks):
+                shift_copy(k, 1).wait_send()
 
         for period in range(TICKS):
             each_tile(period, lambda copy: copy.wait_send(), lambda copy: copy.wait())
@@ -461,6 +489,7 @@
     channels = rows * row_block
     pairs = channels // BLOCK
     width = (2 * pairs + 1) * BLOCK
+    pieces = len(piece_list(2 * pairs)[0])
     assert row_block == BLOCK and TICKS == 2
     vmem = pl.BlockSpec(memory_space=pltpu.VMEM)
     dma = pltpu.SemaphoreType.DMA
@@ -487,12 +516,12 @@
             dma((rows * cols,)),
             dma((2,)),
             dma((2, cols)),
-            dma((TICKS, 2 * pairs)),
-            dma((TICKS, 2, 2 * pairs)),
+            dma((TICKS, pieces)),
+            dma((TICKS, 2, pieces)),
             dma((TICKS, rows * cols)),
             dma((TICKS,)),
-            dma,
-            dma,
+            dma((pairs,)),
+            dma((pairs,)),
         ],
         compiler_params=pltpu.CompilerParams(
             collective_id=0, has_side_effects=True, vmem_limit_bytes=52 * 1024 * 1024

time: 166 us -> 143 us (0.86)
  Pallas kernels: 161 us -> 138 us
    pallas_call x1, Pallas kernels: 161 us -> 138 us  [gather(): pl.pallas_call(functools.partial(gather_kernel, rows, cols, sectors), out...]
where the time goes in v1:
time: 143 us
  Pallas kernels  138 us (97%)
  local copies, waits for them, and re-layouts  2.07 us (1%)
  other arithmetic  1.69 us (1%)
    pallas_call x1, Pallas kernels, gather(): pl.pallas_call(functools.partial(gather_kernel, rows, cols, sectors), out...  138 us

profile of v1, /device:TPU:29, one launch (start us, length us, event | category | flops | bytes accessed | tf_op | source)
XLA Modules:
  0.0 142.8 jit_solution(8769175286946629433)
XLA Ops:
  0.0 0.0 copy-start
  0.0 0.7 dynamic_slice.6
  0.7 0.7 multiply_bitcast_fusion
  1.4 0.6 fusion
  3.3 0.0 copy-done
  3.3 0.1 multiply_divide_fusion
  3.5 0.9 pad_maximum_fusion.tile_ref
  4.4 137.7 %sectors.1 = f32[2,256,128]{2,1,0:T(8,128)S(1)} custom-call(bf16[2,128,4096]{2,1,0:T(8,128)(2,1)} %bitcast.9, f32[8,1024]{1,0:T(8,128)S(1)} %pad.4.weight_ref, f32[2,256,128]{2,1,0:T(8,128)S(1)} %pad_maximum_fusion.tile_ref), custom_call_target="tpu_custom_call" | custom-call | tf_op jit(solution)/shard_map/sectors/pallas_call | solution.py:498
  142.1 0.7 copy.9
  (3 shorter events, 0.0 us)
Async XLA Ops:
  0.0 3.3 %copy-start = (f32[1,4096]{1,0:T(1,128)S(1)}, f32[1,4096]{1,0:T(1,128)}, u32[]{:S(2)}) copy-start(f32[1,4096]{1,0:T(1,128)} %param.7) | copy-start | bytes 49156

commit v2 on v1

--- a/solution.py
+++ b/solution.py
@@ -57,15 +57,14 @@
         cols = [jnp.broadcast_to(u[:, base + q : base + q + 1], (SUB, size)) for q in range(SUB)]
         scale = jnp.zeros((SUB, size), jnp.float32)
         for p in range(SUB):
-            pivot = cols[p][p : p + 1, :]
-            scale = jnp.where(sub_rows == p, pivot, scale)
+            root = lax.rsqrt(cols[p][p : p + 1, :])
+            scale = jnp.where(sub_rows == p, root, scale)
             if p + 1 < SUB:
-                f = jnp.where(sub_rows > p, cols[p] / pivot, 0.0)
+                f = jnp.where(sub_rows > p, cols[p], 0.0) * (root * root)
                 u = u - f * u[p : p + 1, :]
                 v = v - f * v[p : p + 1, :]
                 for q in range(p + 1, SUB):
                     cols[q] = cols[q] - f * cols[q][p : p + 1, :]
-        scale = lax.rsqrt(scale)
         u = u * scale
         v = v * scale
         done.append(v)

time: 143 us -> 142 us (level)
  no operation moved by 1% of the time
where the time goes in v2:
time: 142 us
  Pallas kernels  137 us (96%)
  local copies, waits for them, and re-layouts  2.07 us (1%)
  other arithmetic  1.69 us (1%)
    pallas_call x1, Pallas kernels, gather(): pl.pallas_call(functools.partial(gather_kernel, rows, cols, sectors), out...  137 us

profile of v2, /device:TPU:29, one launch (start us, length us, event | category | flops | bytes accessed | tf_op | source)
XLA Modules:
  0.0 142.0 jit_solution(4890005088023003423)
XLA Ops:
  0.0 0.0 copy-start
  0.0 0.7 dynamic_slice.6
  0.7 0.7 multiply_bitcast_fusion
  1.4 0.6 fusion
  3.3 0.0 copy-done
  3.3 0.1 multiply_divide_fusion
  3.5 0.9 pad_maximum_fusion.tile_ref
  4.4 136.9 %sectors.1 = f32[2,256,128]{2,1,0:T(8,128)S(1)} custom-call(bf16[2,128,4096]{2,1,0:T(8,128)(2,1)} %bitcast.9, f32[8,1024]{1,0:T(8,128)S(1)} %pad.4.weight_ref, f32[2,256,128]{2,1,0:T(8,128)S(1)} %pad_maximum_fusion.tile_ref), custom_call_target="tpu_custom_call" | custom-call | tf_op jit(solution)/shard_map/sectors/pallas_call | solution.py:497
  141.3 0.7 copy.9
  (3 shorter events, 0.0 us)
Async XLA Ops:
  0.0 3.3 %copy-start = (f32[1,4096]{1,0:T(1,128)S(1)}, f32[1,4096]{1,0:T(1,128)}, u32[]{:S(2)}) copy-start(f32[1,4096]{1,0:T(1,128)} %param.7) | copy-start | bytes 49156

commit v3 on v2

--- a/solution.py
+++ b/solution.py
@@ -126,21 +126,23 @@
     my_tile = pl.ds(pl.multiple_of(col * tile_rows, tile_rows), tile_rows)
     source = row * cols + col
 
-    def amp_there(r):
+    def amp_there(d):
+        r = lax.rem(row + d, rows)
         return pltpu.make_async_remote_copy(
-            src_ref=amp_ref.at[:, :, pl.ds(r * chunk, chunk)],
+            src_ref=amp_ref.at[:, :, pl.ds(pl.multiple_of(r * chunk, chunk), chunk)],
             dst_ref=panels.at[:, my_rows, my_states],
-            send_sem=amp_send.at[r],
+            send_sem=amp_send.at[d],
             recv_sem=amp_recv.at[source],
             device_id={"row": r, "col": home},
             device_id_type=MESH,
         )
 
-    def amp_here(r):
+    def amp_here(d):
+        r = lax.rem(row + d, rows)
         return pltpu.make_async_copy(
-            amp_ref.at[:, :, pl.ds(r * chunk, chunk)],
+            amp_ref.at[:, :, pl.ds(pl.multiple_of(r * chunk, chunk), chunk)],
             panels.at[:, my_rows, my_states],
-            amp_send.at[r],
+            amp_send.at[d],
         )
 
     def small_there(src, dst, i):
@@ -167,16 +169,16 @@
         def _():
             small_there(src, dst, i).start()
 
-    for r in range(rows):
-        here = at_home & (row == r)
+    for d in (*range(1, rows), 0):
+        here = at_home & (d == 0)
 
         @pl.when(here)
         def _():
-            amp_here(r).start()
+            amp_here(d).start()
 
         @pl.when(jnp.logical_not(here))
         def _():
-            amp_there(r).start()
+            amp_there(d).start()
 
     for i, (src, dst) in enumerate(smalls):
 
@@ -188,16 +190,16 @@
         def _():
             small_there(src, dst, i).wait_send()
 
-    for r in range(rows):
-        here = at_home & (row == r)
+    for d in (*range(1, rows), 0):
+        here = at_home & (d == 0)
 
         @pl.when(here)
         def _():
-            amp_here(r).wait()
+            amp_here(d).wait()
 
         @pl.when(jnp.logical_not(here))
         def _():
-            amp_there(r).wait_send()
+            amp_there(d).wait_send()
 
     pieces, of_block = piece_list(blocks)
 

time: 142 us -> 142 us (level)
  no operation moved by 1% of the time
where the time goes in v3:
time: 142 us
  Pallas kernels  137 us (96%)
  local copies, waits for them, and re-layouts  2.07 us (1%)
  other arithmetic  1.69 us (1%)
    pallas_call x1, Pallas kernels, gather(): pl.pallas_call(functools.partial(gather_kernel, rows, cols, sectors), out...  137 us

profile of v3, /device:TPU:29, one launch (start us, length us, event | category | flops | bytes accessed | tf_op | source)
XLA Modules:
  0.0 141.9 jit_solution(12178567126010759563)
XLA Ops:
  0.0 0.0 copy-start
  0.0 0.7 dynamic_slice.6
  0.7 0.7 multiply_bitcast_fusion
  1.4 0.6 fusion
  3.3 0.0 copy-done
  3.3 0.1 multiply_divide_fusion
  3.5 0.9 pad_maximum_fusion.tile_ref
  4.4 136.8 %sectors.1 = f32[2,256,128]{2,1,0:T(8,128)S(1)} custom-call(bf16[2,128,4096]{2,1,0:T(8,128)(2,1)} %bitcast.9, f32[8,1024]{1,0:T(8,128)S(1)} %pad.4.weight_ref, f32[2,256,128]{2,1,0:T(8,128)S(1)} %pad_maximum_fusion.tile_ref), custom_call_target="tpu_custom_call" | custom-call | tf_op jit(solution)/shard_map/sectors/pallas_call | solution.py:499
  141.2 0.7 copy.9
  (3 shorter events, 0.0 us)
Async XLA Ops:
  0.0 3.3 %copy-start = (f32[1,4096]{1,0:T(1,128)S(1)}, f32[1,4096]{1,0:T(1,128)}, u32[]{:S(2)}) copy-start(f32[1,4096]{1,0:T(1,128)} %param.7) | copy-start | bytes 49156
